TPU v7x, 256 devices: a whole 4x4x8 slice. The times are simulated.
256 devices in a mesh: users: 64 (over z, x, core), seq: 4 (over y).
Axes of the slice: x: 4, y: 4, z: 8, core: 2. Of those that a mesh axis runs over, the one named last changes fastest.
Arguments:
- tokens: bfloat16 [65536, 1024], P(('users', 'seq')), may hold values from -24 to 24, as said below
- item_table: bfloat16 [16384, 1024], P('users'), may hold values from -24 to 24, as said below
- w_in: bfloat16 [1024, 4096], replicated, may hold values from -0.1875 to 0.1875
- w_out: bfloat16 [1024, 1024], replicated, may hold values from -0.1875 to 0.1875
- gain_in: float32 [1024], replicated, may hold values from 0.25 to 1.75
- gain_attn: float32 [1024], replicated, may hold values from 0.25 to 1.75
- hist_len: int32 [128], P('users'), may hold values from 1 to 896, as said below
- row_start: int32 [128], P('users'), may hold values from 0 to 65408, as said below
- impressions: int32 [128, 1024], P('users', 'seq'), may hold values from 0 to 16383, as said below
- item_slot: int32 [16384], replicated, may hold values from 0 to 16383, as said below
Outputs:
- hist_out: bfloat16 [65536, 1024], P(('users', 'seq'))
- cand_out: bfloat16 [128, 1024, 1024], P('users', 'seq')
Inputs may be any that keep to these rules, and one draw needn't show every extreme that they name: `hist_len`: users 2g and 2g+1 are the histories of users index g; each history of length n fills ceil(n / 128) blocks, and the two together fill all 1024 rows of their users index. row_start[2g] = g * 1024; row_start[2g+1] = row_start[2g] + 128 * ceil(hist_len[2g] / 128). A permutation: item i is row item_slot[i] of item_table, held by users index item_slot[i] // 256. Of the 512 impressions on one device (the users of one users index, the candidates of one seq index), at most 16 are items held by any one users index. Ids may repeat. `tokens`: entries are of order one, with rows and columns of different scales. `item_table`: entries are of order one, with rows and columns of different scales.
All inputs are finite; a program needn't handle non-finite values.
Results may differ from a plain program's by a relative error of at most 0.008.
Values may be sent and summed in bfloat16 or wider, within the bound.
A program may use at most 128 MiB of HBM per device.

v0:
```python
import math

import jax
import jax.numpy as jnp
from jax import lax
from jax.sharding import PartitionSpec as P

HEADS = 8


epsilon = 1e-05


def layer_norm(values, gain_vec):
    centered = values - jnp.mean(values, axis=-1, keepdims=True)
    spread = jnp.mean(centered * centered, axis=-1, keepdims=True)
    return centered * lax.rsqrt(spread + epsilon) * gain_vec


def finish(rows_in, attended, gate_part, gain_attn, w_out):
    mixed_rows = (layer_norm(attended, gain_attn) * gate_part.astype(jnp.float32)).astype(
        jnp.bfloat16
    )
    summed = rows_in.astype(jnp.float32) + jnp.dot(
        mixed_rows, w_out, preferred_element_type=jnp.float32
    )
    return summed.astype(jnp.bfloat16)


def body(
    tokens, item_table, w_in, w_out, gain_in, gain_attn, hist_len, row_start, impressions, item_slot
):
    row_count, model_width = tokens.shape
    head_dim = model_width // HEADS
    scale_factor = 1.0 / math.sqrt(head_dim)
    seq_size = lax.axis_size("seq")
    user_size = lax.axis_size("users")
    group_rows = row_count * seq_size
    row_first = lax.axis_index("seq") * row_count
    group_start = row_start - lax.axis_index("users") * group_rows

    def locate(position):
        row_user = (position >= group_start[1]).astype(jnp.int32)
        row_end = jnp.where(
            row_user == 1, group_start[1] + hist_len[1], group_start[0] + hist_len[0]
        )
        return (row_user, position < row_end)

    w_gate = w_in[:, :model_width]
    w_value = w_in[:, model_width : 2 * model_width]
    w_query = w_in[:, 2 * model_width : 3 * model_width]
    w_key = w_in[:, 3 * model_width :]
    normed = layer_norm(tokens.astype(jnp.float32), gain_in).astype(jnp.bfloat16)
    gate_part = jax.nn.silu(jnp.dot(normed, w_gate, preferred_element_type=jnp.float32)).astype(
        jnp.bfloat16
    )
    query_part = jnp.dot(normed, w_query, preferred_element_type=jnp.float32).astype(jnp.bfloat16)
    wanted = impressions.reshape(-1)
    request_count = wanted.shape[0]
    slot_ids = item_slot[wanted]
    table_rows = item_table.shape[0]
    owner_ids = slot_ids // table_rows
    local_rows = slot_ids - owner_ids * table_rows
    capacity = max(2, 2 * request_count // user_size)
    ordinal = jnp.arange(request_count, dtype=jnp.int32)
    earlier = (owner_ids[:, None] == owner_ids[None, :]) & (ordinal[None, :] < ordinal[:, None])
    slot_rank = jnp.sum(earlier.astype(jnp.int32), axis=1)
    target = owner_ids * capacity + slot_rank
    requests = jnp.full((user_size * capacity,), -1, jnp.int32).at[target].set(local_rows)
    requests = requests.reshape(user_size, capacity)
    looked = item_table[
        jnp.maximum(lax.all_to_all(requests, "users", split_axis=0, concat_axis=0, tiled=True), 0)
    ]
    served = lax.all_to_all(looked, "users", split_axis=0, concat_axis=0, tiled=True)
    embedded = served.reshape(user_size * capacity, model_width)[target]
    cand_normed = layer_norm(embedded.astype(jnp.float32), gain_in).astype(jnp.bfloat16)
    cand_gate = jax.nn.silu(
        jnp.dot(cand_normed, w_gate, preferred_element_type=jnp.float32)
    ).astype(jnp.bfloat16)
    cand_query = jnp.dot(cand_normed, w_query, preferred_element_type=jnp.float32).astype(
        jnp.bfloat16
    )
    cand_user = ordinal // impressions.shape[1]
    query_pos = row_first + jnp.arange(row_count, dtype=jnp.int32)
    query_user, query_live = locate(query_pos)
    query_heads = query_part.reshape(row_count, HEADS, head_dim)
    cand_heads = cand_query.reshape(request_count, HEADS, head_dim)

    def attend(heads_in, key_heads, value_heads, allowed):
        scores = (
            jnp.einsum("qhd,khd->hqk", heads_in, key_heads, preferred_element_type=jnp.float32)
            * scale_factor
        )
        weights = jnp.where(allowed[None], jax.nn.silu(scores), 0.0).astype(jnp.bfloat16)
        return jnp.einsum("hqk,khd->qhd", weights, value_heads, preferred_element_type=jnp.float32)

    value_part = jnp.dot(normed, w_value, preferred_element_type=jnp.float32).astype(jnp.bfloat16)
    key_part = jnp.dot(normed, w_key, preferred_element_type=jnp.float32).astype(jnp.bfloat16)
    keys_in = lax.all_gather(key_part, "seq", axis=0, tiled=True)
    key_count = keys_in.shape[0]
    key_pos = jnp.arange(key_count, dtype=jnp.int32)
    key_user, key_live = locate(key_pos)
    key_heads = keys_in.reshape(key_count, HEADS, head_dim)
    value_heads = lax.all_gather(value_part, "seq", axis=0, tiled=True).reshape(
        key_count, HEADS, head_dim
    )
    causal = (
        (query_user[:, None] == key_user[None, :])
        & query_live[:, None]
        & key_live[None, :]
        & (key_pos[None, :] <= query_pos[:, None])
    )
    visible = (cand_user[:, None] == key_user[None, :]) & key_live[None, :]
    hist_total = attend(query_heads, key_heads, value_heads, causal)
    cand_total = attend(cand_heads, key_heads, value_heads, visible)
    hist_out = finish(
        tokens, hist_total.reshape(row_count, model_width), gate_part, gain_attn, w_out
    )
    cand_out = finish(
        embedded, cand_total.reshape(request_count, model_width), cand_gate, gain_attn, w_out
    )
    return (hist_out, cand_out.reshape(impressions.shape[0], impressions.shape[1], model_width))


def solution(mesh):
    placed = (
        P(("users", "seq"), None),
        P("users", None),
        P(),
        P(),
        P(),
        P(),
        P("users"),
        P("users"),
        P("users", "seq"),
        P(),
    )
    return jax.shard_map(
        body,
        mesh=mesh,
        in_specs=placed,
        out_specs=(P(("users", "seq"), None), P("users", "seq", None)),
        check_vma=False,
    )
```

profile of v0, /device:TPU:64, one launch (start us, length us, event | category | flops | bytes accessed | tf_op | source)
XLA Modules:
  0.0 142.7 jit_solution(11764879104901675190)
XLA Ops:
  7.2 0.0 copy-start
  7.2 0.0 all-gather.3.cloned.1.call-start
  7.2 1.3 convert_reduce_fusion.1
  8.6 1.3 fusion.53
  9.9 0.0 copy-start.3
  9.9 0.0 copy-start.6
  9.9 3.4 %fusion.42 = bf16[256,1024]{1,0:T(8,128)(2,1)} fusion(bf16[1024,4096]{1,0:T(8,128)(2,1)} %param.12, bf16[256,1024]{1,0:T(8,128)(2,1)} %param.10, f32[1024]{0:T(1024)} %param.14, f32[256]{0:T(256)S(1)} %add_rsqrt_fusion.3, f32[256]{0:T(256)S(1)} %broadcast_multiply_fusion.3), kind=kOutput, calls=%fused_computation.47 | convolution fusion | flops 538443776 | bytes 3151872 | tf_op jit(solution)/shard_map/dot_general | solution.py:97
  13.3 0.0 all-gather.3.cloned.1.call-update
  13.3 0.0 copy-start.4
  13.3 0.0 copy-start.2
  13.3 0.0 all-gather.5.cloned.1.call-start
  13.4 0.0 copy-done.3
  13.4 3.2 %fusion.45 = bf16[256,1024]{1,0:T(8,128)(2,1)} fusion(bf16[1024,4096]{1,0:T(8,128)(2,1)} %param.12, bf16[256,1024]{1,0:T(8,128)(2,1)S(1)} %copy-done.3, f32[1024]{0:T(1024)S(1)} %copy-done.6, f32[256]{0:T(256)S(1)} %add_rsqrt_fusion.3, f32[256]{0:T(256)S(1)} %broadcast_multiply_fusion.3), kind=kOutput, calls=%fused_computation.48 | convolution fusion | flops 538443776 | bytes 3151872 | tf_op jit(solution)/shard_map/dot_general | solution.py:98
  16.6 0.0 all-gather.5.cloned.1.call-update
  16.7 3.1 %gather_fusion = s32[512]{0:T(512)S(1)} fusion(s32[16384]{0:T(1024)S(1)} %copy-done.2, s32[1024]{0:T(1024)S(1)} %pad_clamp_fusion.1), kind=kCustom, calls=%fused_computation | custom fusion | bytes 6144 | tf_op jit(solution)/shard_map/gather | solution.py:60
  19.9 0.2 convert_reduce_fusion.2
  20.1 2.4 %scatter_custom_fusion = s32[1024]{0:T(1024)S(1)} fusion(s32[512]{0:T(512)S(1)} %bitcast.78, s32[512]{0:T(512)S(1)} %get-tuple-element.2, s32[]{:T(128)} %constant.73.clone.1), kind=kCustom, calls=%fused_computation.105 | custom fusion | bytes 4100 | tf_op jit(solution)/shard_map/scatter | solution.py:69
  22.6 0.7 all_to_all.9
  23.3 11.1 %all-to-all-start = ((s32[64,1,16]{2,1,0:T(1,128)}), s32[64,1,16]{2,1,0:T(1,128)S(1)}, u32[]{:S(2)}, u32[]{:S(2)}) async-start(s32[64,1,16]{2,1,0:T(1,128)} %bitcast.9), calls=%async_computation | async-start | bytes 65536 | tf_op jit(solution)/shard_map/all_to_all | solution.py:72
  34.4 0.0 copy-done.8
  34.5 0.6 fusion.112
  35.0 7.1 %all-to-all-done = s32[64,1,16]{2,1,0:T(1,128)S(1)} async-done(((s32[64,1,16]{2,1,0:T(1,128)}), s32[64,1,16]{2,1,0:T(1,128)S(1)}, u32[]{:S(2)}, u32[]{:S(2)}) %all-to-all-start) | async-done | bytes 4128 | tf_op jit(solution)/shard_map/all_to_all | solution.py:72
  42.1 0.1 maximum_reduce_fusion
  42.2 0.1 reshape.397
  42.3 5.4 %gather_fusion.1 = bf16[1024,1024]{1,0:T(8,128)(2,1)} fusion(bf16[256,1024]{1,0:T(8,128)(2,1)S(1)} %copy-done.1, s32[1024]{0:T(1024)S(1)} %broadcast_clamp_fusion), kind=kCustom, calls=%fused_computation.1 | custom fusion | bytes 4198400 | tf_op jit(solution)/shard_map/gather | solution.py:71
  47.7 7.4 %all-to-all-start.1 = ((bf16[64,16,1024]{2,1,0:T(8,128)(2,1)}), bf16[64,16,1024]{2,1,0:T(8,128)(2,1)}, u32[]{:S(2)}, u32[]{:S(2)}) async-start(bf16[64,16,1024]{2,1,0:T(8,128)(2,1)} %bitcast.72), calls=%async_computation.1 | async-start | bytes 4194304 | tf_op jit(solution)/shard_map/all_to_all | solution.py:74
  55.2 0.6 fusion.111
  58.2 0.6 compare_convert_fusion
  58.8 0.6 select_compare_fusion
  59.4 0.4 fusion.66
  59.8 1.2 compare_and_fusion
  61.0 3.2 %fusion.50 = bf16[32,8,8,128]{3,2,1,0:T(8,128)(2,1)} fusion(bf16[1024,4096]{1,0:T(8,128)(2,1)} %param.12, bf16[256,1024]{1,0:T(8,128)(2,1)S(1)} %copy-done.3, f32[1024]{0:T(1024)S(1)} %copy-done.6, f32[256]{0:T(256)S(1)} %add_rsqrt_fusion.3, f32[256]{0:T(256)S(1)} %broadcast_multiply_fusion.3), kind=kOutput, calls=%fused_computation.51 | convolution fusion | flops 538443776 | bytes 3151872 | tf_op jit(solution)/shard_map/dot_general | solution.py:57
  64.3 4.0 %copy.46 = bf16[1024,1024]{0,1:T(8,128)(2,1)} copy(bf16[1024,1024]{1,0:T(8,128)(2,1)} %all-gather.3.cloned.1.call-done) | data formatting | bytes 4194304 | tf_op jit(solution)/shard_map/reshape | solution.py:104
  68.2 16.2 %all-gather.5.cloned.1.call-done = bf16[1024,1024]{1,0:T(8,128)(2,1)} async-done(((bf16[256,1024]{1,0:T(8,128)(2,1)}), bf16[1024,1024]{1,0:T(8,128)(2,1)}) %all-gather.5.cloned.1.call-update) | async-done | bytes 2097168 | tf_op jit(solution)/shard_map/all_gather | solution.py:99
  84.4 6.5 %fusion.113 = (f32[256]{0:T(256)S(1)}, f32[8,128,256]{2,1,0:T(8,128)S(1)}) fusion(bf16[1024,8,128]{0,2,1:T(8,128)(2,1)} %bitcast.75, pred[256,1024]{1,0:T(8,128)(4,1)S(1)} %fusion.66, bf16[32,8,8,128]{3,2,1,0:T(8,128)(2,1)} %fusion.50, bf16[1024,1024]{1,0:T(8,128)(2,1)} %all-gather.5.cloned.1.call-done), kind=kOutput, calls=%fused_computation.130 | convolution fusion | flops 1088683776 | bytes 6030336 | tf_op jit(solution)/shard_map/hqk,khd->qhd/dot_general | solution.py:95
  90.9 0.0 copy-start.7
  90.9 1.3 copy.40
  92.3 0.2 fusion.61
  92.5 4.4 %fusion.38 = bf16[256,1024]{1,0:T(8,128)(2,1)} fusion(bf16[1024,1024]{1,0:T(8,128)(2,1)S(1)} %copy-done, bf16[256,1024]{1,0:T(8,128)(2,1)} %param.10, f32[256,1024]{1,0:T(8,128)} %copy.40, bf16[1024,4096]{1,0:T(8,128)(2,1)} %param.12, f32[1024]{0:T(1024)S(1)} %copy-done.7, f32[256]{0:T(256)S(1)} %add_rsqrt_fusion.2, f32[256]{0:T(256)S(1)} %broadcast_multiply_fusion.2, ...), kind=kOutput, calls=%fused_computation.45 | convolution fusion | flops 1078722560 | bytes 6828032 | tf_op jit(solution)/shard_map/dot_general | solution.py:24
  96.9 8.1 %all-to-all-done.1 = bf16[64,16,1024]{2,1,0:T(8,128)(2,1)} async-done(((bf16[64,16,1024]{2,1,0:T(8,128)(2,1)}), bf16[64,16,1024]{2,1,0:T(8,128)(2,1)}, u32[]{:S(2)}, u32[]{:S(2)}) %all-to-all-start.1) | async-done | bytes 2097184 | tf_op jit(solution)/shard_map/all_to_all | solution.py:74
  105.0 4.6 %gather_fusion.2 = bf16[512,1024]{1,0:T(8,128)(2,1)S(1)} fusion(bf16[1024,1024]{1,0:T(8,128)(2,1)} %bitcast.11, s32[1024]{0:T(1024)S(1)} %pad_clamp_fusion), kind=kCustom, calls=%fused_computation.2 | custom fusion | bytes 2099200 | tf_op jit(solution)/shard_map/gather | solution.py:75
  109.6 0.2 convert_reduce_fusion
  109.8 0.4 fusion.6
  110.3 3.9 %fusion.35 = bf16[64,8,8,128]{3,2,1,0:T(8,128)(2,1)} fusion(bf16[1024,4096]{1,0:T(8,128)(2,1)} %param.12, bf16[512,1024]{1,0:T(8,128)(2,1)S(1)} %gather_fusion.2, f32[1024]{0:T(1024)S(1)} %copy-done.6, f32[512]{0:T(512)S(1)} %add_rsqrt_fusion.1, f32[512]{0:T(512)S(1)} %broadcast_multiply_fusion.1), kind=kOutput, calls=%fused_computation.44 | convolution fusion | flops 1076887552 | bytes 4202496 | tf_op jit(solution)/shard_map/dot_general | solution.py:80
  114.1 11.0 %fusion.118 = (f32[512]{0:T(512)S(1)}, f32[8,128,512]{2,1,0:T(8,128)}) fusion(bf16[1024,8,128]{0,2,1:T(8,128)(2,1)} %bitcast.76, pred[512,1024]{1,0:T(8,128)(4,1)} %compare_and_fusion, bf16[64,8,8,128]{3,2,1,0:T(8,128)(2,1)} %fusion.35, bf16[1024,1024]{1,0:T(8,128)(2,1)} %all-gather.5.cloned.1.call-done), kind=kOutput, calls=%fused_computation.131 | convolution fusion | flops 2177367552 | bytes 7866368 | tf_op jit(solution)/shard_map/hqk,khd->qhd/dot_general | solution.py:95
  125.1 2.9 %copy.45 = f32[512,1024]{1,0:T(8,128)} copy(f32[512,1024]{0,1:T(8,128)} %bitcast.73) | data formatting | bytes 4194304 | tf_op jit(solution)/shard_map/reshape | solution.py:120
  128.1 1.9 %fusion.15 = f32[512]{0:T(512)S(1)} fusion(f32[8,128,512]{2,1,0:T(8,128)} %get-tuple-element.11, f32[512]{0:T(512)S(1)} %broadcast_multiply_fusion), kind=kLoop, calls=%fused_computation.22 | loop fusion | flops 1572352 | bytes 2101248 | tf_op jit(solution)/shard_map/reduce_sum | solution.py:16
  129.9 5.9 %fusion.9 = bf16[512,1024]{1,0:T(8,128)(2,1)} fusion(bf16[512,1024]{1,0:T(8,128)(2,1)S(1)} %gather_fusion.2, bf16[1024,1024]{1,0:T(8,128)(2,1)S(1)} %copy-done, f32[512,1024]{1,0:T(8,128)} %copy.45, f32[1024]{0:T(1024)S(1)} %copy-done.7, f32[512]{0:T(512)S(1)} %add_rsqrt_fusion, f32[512]{0:T(512)S(1)} %broadcast_multiply_fusion, ...), kind=kOutput, calls=%fused_computation.17 | convolution fusion | flops 2157445120 | bytes 9453568 | tf_op jit(solution)/shard_map/dot_general | solution.py:24
  (29 shorter events, 0.1 us)
Async XLA Ops:
  7.2 85.3 %copy-start = (bf16[1024,1024]{1,0:T(8,128)(2,1)S(1)}, bf16[1024,1024]{1,0:T(8,128)(2,1)}, u32[]{:S(2)}) copy-start(bf16[1024,1024]{1,0:T(8,128)(2,1)} %param.13) | copy-start | bytes 6291460
  7.2 57.1 %all-gather.3.cloned.1.call-start = ((), (), s32[]{:S(2)}) async-start(), calls=%async_computation.2 | async-start | bytes 2621440 | tf_op jit(solution)/shard_map/all_gather | solution.py:104
  9.9 3.5 %copy-start.3 = (bf16[256,1024]{1,0:T(8,128)(2,1)S(1)}, bf16[256,1024]{1,0:T(8,128)(2,1)}, u32[]{:S(2)}) copy-start(bf16[256,1024]{1,0:T(8,128)(2,1)} %param.10) | copy-start | bytes 1572868
  9.9 3.5 %copy-start.6 = (f32[1024]{0:T(1024)S(1)}, f32[1024]{0:T(1024)}, u32[]{:S(2)}) copy-start(f32[1024]{0:T(1024)} %param.14) | copy-start | bytes 12292
  13.3 3.3 %copy-start.4 = (s32[2,256]{1,0:T(2,128)S(1)}, s32[2,256]{1,0:T(2,128)}, u32[]{:S(2)}) copy-start(s32[2,256]{1,0:T(2,128)} %param.18) | copy-start | bytes 6148
  13.3 3.3 %copy-start.2 = (s32[16384]{0:T(1024)S(1)}, s32[16384]{0:T(1024)}, u32[]{:S(2)}) copy-start(s32[16384]{0:T(1024)} %param.19) | copy-start | bytes 196612
  13.3 71.1 %all-gather.5.cloned.1.call-start = ((), (), s32[]{:S(2)}) async-start(), calls=%async_computation.3 | async-start | bytes 2621440 | tf_op jit(solution)/shard_map/all_gather | solution.py:99
  16.6 17.8 %copy-start.8 = (s32[2]{0:T(128)S(1)}, s32[2]{0:T(128)}, u32[]{:S(2)}) copy-start(s32[2]{0:T(128)} %param.17) | copy-start | bytes 28
  16.6 25.7 %copy-start.1 = (bf16[256,1024]{1,0:T(8,128)(2,1)S(1)}, bf16[256,1024]{1,0:T(8,128)(2,1)}, u32[]{:S(2)}) copy-start(bf16[256,1024]{1,0:T(8,128)(2,1)} %param.11) | copy-start | bytes 1572868
  23.3 18.9 %all-to-all-start = ((s32[64,1,16]{2,1,0:T(1,128)}), s32[64,1,16]{2,1,0:T(1,128)S(1)}, u32[]{:S(2)}, u32[]{:S(2)}) async-start(s32[64,1,16]{2,1,0:T(1,128)} %bitcast.9), calls=%async_computation | async-start | bytes 65536 | tf_op jit(solution)/shard_map/all_to_all | solution.py:72
  47.7 7.4 %copy-start.5 = (s32[2]{0:T(128)S(1)}, s32[2]{0:T(128)}, u32[]{:S(2)}) copy-start(s32[2]{0:T(128)} %param.16) | copy-start | bytes 28
  47.7 57.3 %all-to-all-start.1 = ((bf16[64,16,1024]{2,1,0:T(8,128)(2,1)}), bf16[64,16,1024]{2,1,0:T(8,128)(2,1)}, u32[]{:S(2)}, u32[]{:S(2)}) async-start(bf16[64,16,1024]{2,1,0:T(8,128)(2,1)} %bitcast.72), calls=%async_computation.1 | async-start | bytes 4194304 | tf_op jit(solution)/shard_map/all_to_all | solution.py:74
  90.9 1.5 %copy-start.7 = (f32[1024]{0:T(1024)S(1)}, f32[1024]{0:T(1024)}, u32[]{:S(2)}) copy-start(f32[1024]{0:T(1024)} %param.15) | copy-start | bytes 12292
Sparse Core Ops, SparseCore 0:
  13.4 35.6 all-gather.2
  50.9 33.4 all-gather.4
where the time goes:
time: 146 us; the launch traced here: 143 us
  matrix products  41.5 us (28%)
  waiting for transfers between devices  31.5 us (22%)
  local copies, waits for them, and re-layouts  25.7 us (18%)
  starting transfers between devices  18.6 us (13%)
  between operations  16.8 us (12%)
  other arithmetic  8.56 us (6%)
    dot_general x2, matrix products, attend(): jnp.einsum('hqk,khd->qhd', weights, value_heads, preferred_element_type=j...  17.5 us
    all_gather x1, waiting for transfers between devices, body(): keys_in = lax.all_gather(key_part, 'seq', axis=0, tiled=True)  16.2 us
    all_to_all x1, starting transfers between devices, body(): lax.all_to_all(requests, 'users', split_axis=0, concat_axis=0, tiled=True)  11.1 us
    dot_general x2, matrix products, finish(): jnp.dot(mixed_rows, w_out, preferred_element_type=jnp.float32)  10.4 us
    all_to_all x1, waiting for transfers between devices, body(): lax.all_to_all(looked, 'users', split_axis=0, concat_axis=0, tiled=True)  8.14 us
    all_to_all x1, starting transfers between devices, body(): lax.all_to_all(looked, 'users', split_axis=0, concat_axis=0, tiled=True)  7.43 us
    all_to_all x1, waiting for transfers between devices, body(): lax.all_to_all(requests, 'users', split_axis=0, concat_axis=0, tiled=True)  7.13 us
    gather x1, local copies, waits for them, and re-layouts, body(): item_table[jnp.maximum(lax.all_to_all(requests, 'users', split_axis=0, co...  5.37 us
  transfers between devices with their start and end apart: 4, of which 3 were waited for; matrix products, arithmetic and copies ran while one was open for 27% of the time, Pallas kernels for 0%

commit v1 on v0

v1 whole, which is shorter than its diff:
```python
import functools
import math

import jax
import jax.numpy as jnp
from jax import lax
from jax.experimental import pallas as pl
from jax.experimental.pallas import tpu as pltpu
from jax.sharding import PartitionSpec as P

MESH = pl.DeviceIdType.MESH
HEADS = 8
WIDTH = 1024
HEAD_DIM = WIDTH // HEADS
ROWS = 256
CANDS = 512
KEYS = 1024
CAP = 16
OWNERS = 64
CHUNK = 128
epsilon = 1e-05
F32 = jnp.float32
BF16 = jnp.bfloat16
I32 = jnp.int32


def group_dz(q):
    return [0, 1, 7, 2, 6, 3, 5, 4][q]


def group_of_dz(dz):
    return jnp.where(dz == 0, 0, jnp.where(dz <= 4, 2 * dz - 1, 2 * (8 - dz)))


def layer_norm(values, gain_row):
    centered = values - jnp.mean(values, axis=-1, keepdims=True)
    spread = jnp.mean(centered * centered, axis=-1, keepdims=True)
    return centered * lax.rsqrt(spread + epsilon) * gain_row


def half_silu(half):
    return half + half * jnp.tanh(half)


def dot(a, b):
    return jnp.dot(a, b, preferred_element_type=F32)


def dot_nt(a, b):
    return lax.dot_general(a, b, (((1,), (1,)), ((), ())), preferred_element_type=F32)


def dot_tn(a, b):
    return lax.dot_general(a, b, (((0,), (0,)), ((), ())), preferred_element_type=F32)


def iota(shape, dim):
    return lax.broadcasted_iota(I32, shape, dim)


def kernel(
    hist_len, row_start, tokens, table, w_in, w_out, gain_in, gain_attn, wanted, item_slot,
    hist_out, cand_out,
    win, wout, normed, keys, values, hgate, hquery, attended, scale_mask,
    requests, asked, served, embedded, cgate, cquery, csorted, place,
    w_sem, req_send, req_recv, row_send, row_recv, ring_send, ring_recv,
):
    me = lax.axis_index("users")
    y = lax.axis_index("seq")
    z, x, c = me // 8, (me // 2) % 4, me % 2
    half_scale = 0.5 / math.sqrt(HEAD_DIM)

    def device(zz, xx, cc, yy):
        return {"users": ((zz + 8) % 8) * 8 + ((xx + 4) % 4) * 2 + (cc + 2) % 2, "seq": (yy + 4) % 4}

    def remote(src, dst, send, recv, target):
        return pltpu.make_async_remote_copy(
            src_ref=src, dst_ref=dst, send_sem=send, recv_sem=recv, device_id=target, device_id_type=MESH
        )

    weight_copies = [
        pltpu.make_async_copy(w_in.at[:, pl.ds(b * WIDTH, WIDTH)], win.at[b], w_sem.at[b]) for b in range(4)
    ]
    weight_copies.append(pltpu.make_async_copy(w_out, wout, w_sem.at[4]))
    for copy in weight_copies:
        copy.start()

    barrier = pltpu.get_barrier_semaphore()
    for q in range(8):
        for k in range(8):
            if q or k:
                pl.semaphore_signal(
                    barrier, inc=1, device_id=device(z + group_dz(q), x + k // 2, c + k % 2, y), device_id_type=MESH
                )
    for dy in (1, 3):
        pl.semaphore_signal(barrier, inc=1, device_id=device(z, x, c, y + dy), device_id_type=MESH)

    ids = jnp.concatenate([wanted[0:1, :], wanted[1:2, :]], axis=1)
    pick_high = (iota((128, CANDS), 0) == (ids >> 7)).astype(BF16)
    slots_2d = item_slot[...]
    at_high = dot_tn((slots_2d >> 7).astype(F32).astype(BF16), pick_high) * 128.0 + dot_tn(
        (slots_2d & 127).astype(F32).astype(BF16), pick_high
    )
    slot = jnp.sum(jnp.where(iota((128, CANDS), 0) == (ids & 127), at_high, 0.0), axis=0, keepdims=True)
    slot = slot.astype(I32)
    owner, local = slot >> 8, slot & 255
    dz = ((owner >> 3) - z) & 7
    dx = (((owner >> 1) & 3) - x) & 3
    dc = (owner - c) & 1
    lot = group_of_dz(dz) * 8 + dx * 2 + dc
    is_lot = iota((OWNERS, CANDS), 0) == lot
    lot_hot = is_lot.astype(BF16)
    earlier = (iota((CANDS, CANDS), 0) < iota((CANDS, CANDS), 1)).astype(BF16)
    before = dot(lot_hot, earlier)
    total = jnp.sum(is_lot.astype(F32), axis=1, keepdims=True)
    rank = jnp.sum(jnp.where(is_lot, before, 0.0), axis=0, keepdims=True).astype(I32)
    base = jnp.sum(jnp.where(iota((OWNERS, CANDS), 0) < lot, total, 0.0), axis=0, keepdims=True)
    position = base.astype(I32) + rank
    lane = (lot & 7) * CAP + rank
    lane_local = jnp.where(iota((128, CANDS), 0) == lane, local, 0).astype(F32).astype(BF16)
    request_rows = dot_nt(lot_hot, lane_local).astype(I32)
    for j in range(OWNERS):
        requests[j] = request_rows[j : j + 1, :]
    asked[0] = request_rows[0:1, :]

    normed[y] = layer_norm(tokens[...].astype(F32), gain_in[...]).astype(BF16)

    pl.semaphore_wait(barrier, 65)

    for q in range(8):
        for k in range(8):
            if q or k:
                j = q * 8 + k
                remote(
                    requests.at[j], asked.at[j], req_send, req_recv.at[q],
                    device(z + group_dz(q), x + k // 2, c + k % 2, y),
                ).start()
    up, down = device(z, x, c, y + 1), device(z, x, c, y - 1)
    own, below, above = normed.at[y], normed.at[(y + 3) % 4], normed.at[(y + 1) % 4]
    remote(own, own, ring_send.at[0], ring_recv.at[0], up).start()
    remote(own, own, ring_send.at[1], ring_recv.at[1], down).start()

    slot_user = lot * CAP + rank + jnp.where(iota((1, CANDS), 1) >= CANDS // 2, 1024, 0)
    sorted_slot = jnp.sum(
        jnp.where(iota((CANDS, CANDS), 0) == position, slot_user, 0).astype(F32), axis=1, keepdims=True
    ).astype(I32)
    position_column = jnp.sum(
        jnp.where(iota((CANDS, CANDS), 0) == iota((CANDS, CANDS), 1), position, 0).astype(F32),
        axis=1,
        keepdims=True,
    ).astype(I32)
    place[:, 0:1] = sorted_slot
    place[:, 1:2] = position_column

    for q in range(8):
        first = 1 if q == 0 else 0
        lots = pl.ds(q * 8 + first, 8 - first)
        remote(asked.at[lots], asked.at[lots], req_send, req_recv.at[q], up).wait_recv()
        gathered = asked[q * 8]
        for k in range(1, 8):
            gathered = gathered + asked[q * 8 + k]
        pick = (iota((ROWS, CHUNK), 0) == gathered).astype(BF16)
        served[pl.ds(q * CHUNK, CHUNK), :] = dot_tn(pick, table[...]).astype(BF16)
        for k in range(first, 8):
            rows = pl.ds(q * CHUNK + k * CAP, CAP)
            remote(
                served.at[rows], embedded.at[rows], row_send, row_recv.at[q],
                device(z - group_dz(q), x - k // 2, c - k % 2, y),
            ).start()
    embedded[pl.ds(0, CAP), :] = served[pl.ds(0, CAP), :]

    def project(rows_value, block, write):
        def step(n, carry):
            columns = pl.ds(pl.multiple_of(n * 256, 256), 256)
            write(columns, dot(rows_value(), win[block, :, columns]))
            return carry

        lax.fori_loop(0, WIDTH // 256, step, 0)

    def project_keys(block):
        rows = pl.ds(pl.multiple_of(block * ROWS, ROWS), ROWS)

        def write_value(columns, out):
            values[rows, columns] = out.astype(BF16)

        def write_key(columns, out):
            keys[rows, columns] = out.astype(BF16)

        project(lambda: normed[block], 1, write_value)
        project(lambda: normed[block], 3, write_key)

    def write_hgate(columns, out):
        hgate[:, columns] = half_silu(out * 0.5).astype(BF16)

    def write_hquery(columns, out):
        hquery[:, columns] = out.astype(BF16)

    for copy in weight_copies:
        copy.wait()
    project(lambda: normed[y], 0, write_hgate)
    project(lambda: normed[y], 2, write_hquery)
    project_keys(y)

    upper, lower = pl.ds(0, ROWS // 2), pl.ds(ROWS // 2, ROWS // 2)
    remote(below, below, ring_send.at[0], ring_recv.at[0], up).wait()
    remote(below.at[upper], below.at[upper], ring_send.at[0], ring_recv.at[2], up).start()
    remote(above, above, ring_send.at[1], ring_recv.at[1], down).wait()
    remote(above.at[lower], above.at[lower], ring_send.at[1], ring_recv.at[3], down).start()
    project_keys((y + 3) % 4)
    project_keys((y + 1) % 4)
    far = normed.at[(y + 2) % 4]
    remote(below.at[upper], far.at[upper], ring_send.at[0], ring_recv.at[2], up).wait()
    remote(above.at[lower], far.at[lower], ring_send.at[1], ring_recv.at[3], down).wait()
    project_keys((y + 2) % 4)

    group_base = me * KEYS
    second = row_start[1] - group_base
    end_first, end_second = row_start[0] - group_base + hist_len[0], second + hist_len[1]

    def locate(spot):
        user = (spot >= second).astype(I32)
        return user, spot < jnp.where(user == 1, end_second, end_first)

    key_spot = iota((1, KEYS), 1)
    key_user, key_live = locate(key_spot)
    query_spot = y * ROWS + iota((ROWS, 1), 0)
    query_user, query_live = locate(query_spot)

    def attend(rows, query):
        def head(h, carry):
            columns = pl.ds(pl.multiple_of(h * HEAD_DIM, HEAD_DIM), HEAD_DIM)
            scores = dot_nt(query[:, columns], keys[:, columns])
            weights = half_silu(scores * scale_mask[0:rows, :]).astype(BF16)
            attended[0:rows, columns] = dot(weights, values[:, columns])
            return carry

        lax.fori_loop(0, HEADS, head, 0)

    def finish(rows, residual, gate, write):
        mixed = (layer_norm(attended[0:rows, :], gain_attn[...]) * gate[...].astype(F32)).astype(BF16)
        for n in range(WIDTH // 256):
            columns = pl.ds(n * 256, 256)
            write(columns, (residual(columns) + dot(mixed, wout[:, columns])).astype(BF16))

    allowed = (
        (query_user == key_user)
        & (query_live & key_live)
        & (key_spot <= query_spot)
    )
    scale_mask[...] = jnp.where(allowed, half_scale, 0.0)
    attend(ROWS, hquery)

    def write_hist(columns, out):
        hist_out[:, columns] = out

    finish(ROWS, lambda columns: tokens[:, columns].astype(F32), hgate, write_hist)

    def wait_group(q):
        rows = pl.ds(CAP, CHUNK - CAP) if q == 0 else pl.ds(q * CHUNK, CHUNK)
        remote(embedded.at[rows], embedded.at[rows], row_send, row_recv.at[q], up).wait_recv()

    for q in range(4):
        wait_group(q)
    for piece in range(4):
        wait_group(piece + 4)
        slot_column = place[pl.ds(piece * CHUNK, CHUNK), 0:1]
        pick = (iota((CHUNK, 5 * CHUNK), 1) + piece * CHUNK == (slot_column & 1023)).astype(BF16)
        rows_in = dot(pick, embedded[pl.ds(piece * CHUNK, 5 * CHUNK), :])
        cand_normed = layer_norm(rows_in, gain_in[...]).astype(BF16)
        for n in range(WIDTH // 256):
            columns = pl.ds(n * 256, 256)
            cgate[:, columns] = half_silu(dot(cand_normed, win[0, :, columns]) * 0.5).astype(BF16)
            cquery[:, columns] = dot(cand_normed, win[2, :, columns]).astype(BF16)
        visible = ((slot_column >> 10) == key_user) & key_live
        scale_mask[0:CHUNK, :] = jnp.where(visible, half_scale, 0.0)
        attend(CHUNK, cquery)

        def write_sorted(columns, out, piece=piece):
            csorted[pl.ds(piece * CHUNK, CHUNK), columns] = out

        finish(CHUNK, lambda columns, rows_in=rows_in: rows_in[:, columns.start : columns.start + 256], cgate, write_sorted)

    for half in range(2):
        spots = place[pl.ds(half * 256, 256), 1:2]
        unpick = (iota((256, CANDS), 1) == spots).astype(BF16)
        cand_out[half] = dot(unpick, csorted[...]).astype(BF16)

    lots = pl.ds(1, OWNERS - 1)
    remote(requests.at[lots], requests.at[lots], req_send, req_recv.at[0], up).wait_send()
    rows = pl.ds(CAP, 1024 - CAP)
    remote(served.at[rows], served.at[rows], row_send, row_recv.at[0], up).wait_send()


def body(
    tokens, item_table, w_in, w_out, gain_in, gain_attn, hist_len, row_start, impressions, item_slot
):
    vmem = pl.BlockSpec(memory_space=pltpu.VMEM)
    smem = pl.BlockSpec(memory_space=pltpu.SMEM)
    anywhere = pl.BlockSpec(memory_space=pl.ANY)
    return pl.pallas_call(
        kernel,
        out_shape=(
            jax.ShapeDtypeStruct((ROWS, WIDTH), BF16),
            jax.ShapeDtypeStruct((2, CANDS // 2, WIDTH), BF16),
        ),
        in_specs=[smem, smem, vmem, vmem, anywhere, anywhere, vmem, vmem, vmem, vmem],
        out_specs=(vmem, vmem),
        scratch_shapes=[
            pltpu.VMEM((4, WIDTH, WIDTH), BF16),
            pltpu.VMEM((WIDTH, WIDTH), BF16),
            pltpu.VMEM((4, ROWS, WIDTH), BF16),
            pltpu.VMEM((KEYS, WIDTH), BF16),
            pltpu.VMEM((KEYS, WIDTH), BF16),
            pltpu.VMEM((ROWS, WIDTH), BF16),
            pltpu.VMEM((ROWS, WIDTH), BF16),
            pltpu.VMEM((ROWS, WIDTH), F32),
            pltpu.VMEM((ROWS, KEYS), F32),
            pltpu.VMEM((OWNERS, 1, 128), I32),
            pltpu.VMEM((OWNERS, 1, 128), I32),
            pltpu.VMEM((OWNERS * CAP, WIDTH), BF16),
            pltpu.VMEM((OWNERS * CAP, WIDTH), BF16),
            pltpu.VMEM((CHUNK, WIDTH), BF16),
            pltpu.VMEM((CHUNK, WIDTH), BF16),
            pltpu.VMEM((CANDS, WIDTH), BF16),
            pltpu.VMEM((CANDS, 128), I32),
            pltpu.SemaphoreType.DMA((5,)),
            pltpu.SemaphoreType.DMA,
            pltpu.SemaphoreType.DMA((8,)),
            pltpu.SemaphoreType.DMA,
            pltpu.SemaphoreType.DMA((8,)),
            pltpu.SemaphoreType.DMA((2,)),
            pltpu.SemaphoreType.DMA((4,)),
        ],
        compiler_params=pltpu.CompilerParams(
            collective_id=0, has_side_effects=True, vmem_limit_bytes=56 * 2**20
        ),
    )(
        hist_len, row_start, tokens, item_table, w_in, w_out,
        gain_in.reshape(1, WIDTH), gain_attn.reshape(1, WIDTH),
        impressions, item_slot.reshape(128, 128),
    )


def solution(mesh):
    placed = (
        P(("users", "seq"), None),
        P("users", None),
        P(),
        P(),
        P(),
        P(),
        P("users"),
        P("users"),
        P("users", "seq"),
        P(),
    )
    return jax.shard_map(
        body,
        mesh=mesh,
        in_specs=placed,
        out_specs=(P(("users", "seq"), None), P("users", "seq", None)),
        check_vma=False,
    )
```

time: 146 us -> 87.1 us (0.60)
  the two profiles are of different devices: /device:TPU:64 before, /device:TPU:49 now
where the time goes in v1:
time: 87.1 us; the launch traced here: 86.9 us
  Pallas kernels  82.2 us (94%)
  local copies, waits for them, and re-layouts  4.13 us (5%)
    pallas_call x1, Pallas kernels, body(): pl.pallas_call(kernel, out_shape=(jax.ShapeDtypeStruct((ROWS, WIDTH), BF1...  82.2 us
    unnamed x2, local copies, waits for them, and re-layouts  4.13 us

profile of v1, /device:TPU:49, one launch (start us, length us, event | category | flops | bytes accessed | tf_op | source)
XLA Modules:
  0.0 86.9 jit_solution(15462018481524613790)
XLA Ops:
  0.6 82.2 %shard_map.113 = (bf16[256,1024]{1,0:T(8,128)(2,1)}, bf16[2,256,1024]{2,1,0:T(8,128)(2,1)}) custom-call(s32[2]{0:T(128)} %hist_len.1, s32[2]{0:T(128)} %row_start.1, bf16[256,1024]{1,0:T(8,128)(2,1)} %tokens.1, bf16[256,1024]{1,0:T(8,128)(2,1)} %table.1, bf16[1024,4096]{1,0:T(8,128)(2,1)} %w_in.1, bf16[1024,1024]{1,0:T(8,128)(2,1)} %w_out.1, ...), custom_call_target="tpu_custom_call" | custom-call | tf_op jit(solution)/shard_map/pallas_call | solution.py:300
  82.8 1.9 %copy.14 = bf16[256,1024]{1,0:T(8,128)(2,1)} copy(bf16[256,1024]{1,0:T(8,128)(2,1)} %get-tuple-element.4) | data formatting | bytes 1048576
  84.7 2.3 %copy.15 = bf16[2,256,1024]{2,1,0:T(8,128)(2,1)} copy(bf16[2,256,1024]{2,1,0:T(8,128)(2,1)} %get-tuple-element.5) | data formatting | bytes 2097152

commit v2 on v1

v2 whole, which is shorter than its diff:
```python
import functools
import math

import jax
import jax.numpy as jnp
from jax import lax
from jax.experimental import pallas as pl
from jax.experimental.pallas import tpu as pltpu
from jax.sharding import PartitionSpec as P

MESH = pl.DeviceIdType.MESH
HEADS = 8
WIDTH = 1024
HEAD_DIM = WIDTH // HEADS
ROWS = 256
CANDS = 512
KEYS = 1024
CAP = 16
OWNERS = 64
NEAR = 5
CHUNK = 128
epsilon = 1e-05
F32 = jnp.float32
BF16 = jnp.bfloat16
I32 = jnp.int32


def group_dz(q):
    return [0, 1, 7, 2, 6, 3, 5, 4][q]


def group_of_dz(dz):
    return jnp.where(dz == 0, 0, jnp.where(dz <= 4, 2 * dz - 1, 2 * (8 - dz)))


def layer_norm(values, gain_row):
    centered = values - jnp.mean(values, axis=-1, keepdims=True)
    spread = jnp.mean(centered * centered, axis=-1, keepdims=True)
    return centered * lax.rsqrt(spread + epsilon) * gain_row


def half_silu(half):
    return half + half * jnp.tanh(half)


def dot(a, b):
    return jnp.dot(a, b, preferred_element_type=F32)


def dot_nt(a, b):
    return lax.dot_general(a, b, (((1,), (1,)), ((), ())), preferred_element_type=F32)


def dot_tn(a, b):
    return lax.dot_general(a, b, (((0,), (0,)), ((), ())), preferred_element_type=F32)


def iota(shape, dim):
    return lax.broadcasted_iota(I32, shape, dim)


def kernel(
    hist_len, row_start, tokens, table, w_in, w_out, gain_in, gain_attn, wanted, item_slot,
    hist_done, keys_done, values_done, rows_done, gate_done, query_done,
    win, wout, normed, keys, values, hgate, hquery, attended, scale_mask, hist,
    requests, asked, asked_far, far_table, served, served_far, embedded,
    rows_in, rows_out, cnormed, cgate, cquery, place,
    w_sem, req_send, req_recv, far_req_recv, row_send, far_row_send, row_recv,
    ring_send, ring_recv, copy_up, copy_down, copy_recv, out_sem,
):
    me = lax.axis_index("users")
    y = lax.axis_index("seq")
    z, x, c = me // 8, (me // 2) % 4, me % 2
    half_scale = 0.5 / math.sqrt(HEAD_DIM)

    def device(zz, xx, cc, yy):
        return {"users": ((zz + 8) % 8) * 8 + ((xx + 4) % 4) * 2 + (cc + 2) % 2, "seq": (yy + 4) % 4}

    def remote(src, dst, send, recv, target):
        return pltpu.make_async_remote_copy(
            src_ref=src, dst_ref=dst, send_sem=send, recv_sem=recv, device_id=target, device_id_type=MESH
        )

    weight_copies = [
        pltpu.make_async_copy(w_in.at[:, pl.ds(b * WIDTH, WIDTH)], win.at[b], w_sem.at[b]) for b in range(4)
    ]
    weight_copies.append(pltpu.make_async_copy(w_out, wout, w_sem.at[4]))
    for copy in weight_copies:
        copy.start()

    barrier = pltpu.get_barrier_semaphore()
    def greet(target):
        pl.semaphore_signal(barrier, inc=1, device_id=target, device_id_type=MESH)

    for q in range(NEAR):
        for k in range(8):
            if q or k:
                greet(device(z + group_dz(q), x + k // 2, c + k % 2, y))
    for dy in (1, 2, 3):
        for k in range(8):
            greet(device(z, x + k // 2, c + k % 2, y + dy))
    greet(device(z + 3, x, c, y))
    greet(device(z + 5, x, c, y))

    ids = jnp.concatenate([wanted[0:1, :], wanted[1:2, :]], axis=1)
    pick_high = (iota((128, CANDS), 0) == (ids >> 7)).astype(BF16)
    slots_2d = item_slot[...]
    at_high = dot_tn((slots_2d >> 7).astype(F32).astype(BF16), pick_high) * 128.0 + dot_tn(
        (slots_2d & 127).astype(F32).astype(BF16), pick_high
    )
    slot = jnp.sum(jnp.where(iota((128, CANDS), 0) == (ids & 127), at_high, 0.0), axis=0, keepdims=True)
    slot = slot.astype(I32)
    owner, local = slot >> 8, slot & 255
    dz = ((owner >> 3) - z) & 7
    dx = (((owner >> 1) & 3) - x) & 3
    dc = (owner - c) & 1
    lot = group_of_dz(dz) * 8 + dx * 2 + dc
    is_lot = iota((OWNERS, CANDS), 0) == lot
    lot_hot = is_lot.astype(BF16)
    earlier = (iota((CANDS, CANDS), 0) < iota((CANDS, CANDS), 1)).astype(BF16)
    before = dot(lot_hot, earlier)
    rank = jnp.sum(jnp.where(is_lot, before, 0.0), axis=0, keepdims=True).astype(I32)
    lane = (lot & 7) * CAP + rank
    lane_local = jnp.where(iota((128, CANDS), 0) == lane, local, 0).astype(F32).astype(BF16)
    request_rows = dot_nt(lot_hot, lane_local).astype(I32)
    for j in range(OWNERS):
        requests[j] = request_rows[j : j + 1, :]
    asked[0] = request_rows[0:1, :]

    normed[y] = layer_norm(tokens[...].astype(F32), gain_in[...]).astype(BF16)

    pl.semaphore_wait(barrier, 65)

    for q in range(8):
        dz = group_dz(q)
        if q < NEAR:
            for k in range(8):
                if q or k:
                    j = q * 8 + k
                    remote(
                        requests.at[j], asked.at[j], req_send, req_recv.at[q],
                        device(z + dz, x + k // 2, c + k % 2, y),
                    ).start()
        else:
            holder_y = (z + dz) % 4
            for k in range(8):
                j = q * 8 + k

                def ask(j=j, k=k, holder_y=holder_y, dz=dz):
                    remote(
                        requests.at[j], asked_far.at[y * 8 + k], req_send, far_req_recv,
                        device(z, x + k // 2, c + k % 2, holder_y),
                    ).start()

                if k:
                    ask()
                else:
                    pl.when(holder_y != y)(ask)

                    @pl.when(holder_y == y)
                    def _(j=j):
                        asked_far[y * 8] = requests[j]

    phase = (z + 8 - y) % 4
    is_holder = phase != 2
    first_half, last_half = pl.ds(0, ROWS // 2), pl.ds(ROWS // 2, ROWS // 2)
    z_up, z_down = device(z + 1, x, c, y), device(z - 1, x, c, y)

    @pl.when(phase == 0)
    def _():
        far_up, far_down = device(z + 3, x, c, y), device(z - 3, x, c, y)
        remote(table.at[first_half], far_table.at[first_half], copy_up, copy_recv.at[0], far_up).start()
        remote(table.at[last_half], far_table.at[last_half], copy_down, copy_recv.at[0], far_down).start()
        remote(table.at[last_half], far_table.at[last_half], copy_up, copy_recv.at[1], far_up).start()
        remote(table.at[first_half], far_table.at[first_half], copy_down, copy_recv.at[1], far_down).start()

    up = device(z, x, c, y + 1)
    own = normed.at[y]
    for dy in (1, 3, 2):
        remote(own, own, ring_send, ring_recv.at[dy - 1], device(z, x, c, y + dy)).start()

    place[:, 0:1] = jnp.sum(
        jnp.where(iota((CANDS, CANDS), 0) == iota((CANDS, CANDS), 1), lot * CAP + rank, 0).astype(F32),
        axis=1,
        keepdims=True,
    ).astype(I32)

    def gather(source, ask, first):
        gathered = ask[first]
        for k in range(1, 8):
            gathered = gathered + ask[first + k]
        pick = (iota((ROWS, CHUNK), 0) == gathered).astype(BF16)
        return dot_tn(pick, source[...]).astype(BF16)

    def send_near(q, k):
        rows = pl.ds(q * CHUNK + k * CAP, CAP)
        remote(
            served.at[rows], embedded.at[rows], row_send, row_recv.at[q],
            device(z - group_dz(q), x - k // 2, c - k % 2, y),
        ).start()

    for q in range(NEAR):
        first = 1 if q == 0 else 0
        lots = pl.ds(q * 8 + first, 8 - first)
        remote(asked.at[lots], asked.at[lots], req_send, req_recv.at[q], up).wait_recv()
        served[pl.ds(q * CHUNK, CHUNK), :] = gather(table, asked, q * 8)
        if q == 0:
            for k in range(1, 8):
                send_near(0, k)
            embedded[pl.ds(0, CAP), :] = served[pl.ds(0, CAP), :]

    @pl.when(phase == 3)
    def _():
        half = far_table.at[first_half]
        remote(half, half, copy_up, copy_recv.at[0], z_up).wait_recv()
        remote(half, half, copy_up, copy_recv.at[0], z_up).start()

    @pl.when(phase == 1)
    def _():
        half = far_table.at[last_half]
        remote(half, half, copy_down, copy_recv.at[0], z_down).wait_recv()
        remote(half, half, copy_down, copy_recv.at[1], z_down).start()

    def project(rows_value, block, write):
        def step(n, carry):
            columns = pl.ds(pl.multiple_of(n * 256, 256), 256)
            write(columns, dot(rows_value(), win[block, :, columns]))
            return carry

        lax.fori_loop(0, WIDTH // 256, step, 0)

    def project_keys(block):
        rows = pl.ds(pl.multiple_of(block * ROWS, ROWS), ROWS)

        def write_value(columns, out):
            values[rows, columns] = out.astype(BF16)

        def write_key(columns, out):
            keys[rows, columns] = out.astype(BF16)

        project(lambda: normed[block], 1, write_value)
        project(lambda: normed[block], 3, write_key)

    def write_hgate(columns, out):
        hgate[:, columns] = half_silu(out * 0.5).astype(BF16)

    def write_hquery(columns, out):
        hquery[:, columns] = out.astype(BF16)

    for copy in weight_copies:
        copy.wait()
    project(lambda: normed[y], 0, write_hgate)
    project(lambda: normed[y], 2, write_hquery)
    project_keys(y)

    @pl.when(phase == 0)
    def _():
        half, other = far_table.at[first_half], far_table.at[last_half]
        remote(half, half, copy_up, copy_recv.at[0], z_up).wait_recv()
        remote(other, other, copy_up, copy_recv.at[1], z_up).wait_recv()

    @pl.when(phase % 2 == 1)
    def _():
        half = far_table.at[first_half]
        remote(half, half, copy_up, copy_recv.at[1], z_up).wait_recv()

    far_group = jnp.where(phase == 0, 7, jnp.where(phase == 3, 6, 5))
    far_base = pl.multiple_of(far_group * CHUNK, CHUNK)

    @pl.when(is_holder)
    def _():
        lots = asked_far.at[pl.ds(0, 31)]
        remote(lots, lots, req_send, far_req_recv, up).wait_recv()
        for dy in range(4):
            served_far[pl.ds(dy * CHUNK, CHUNK), :] = gather(far_table, asked_far, (y + dy) % 4 * 8)
        embedded[pl.ds(far_base, CAP), :] = served_far[0:CAP, :]

    for k in range(8):
        for q in range(1, NEAR):
            send_near(q, k)
            dy = q - 1
            if dy or k:

                @pl.when(is_holder)
                def _(dy=dy, k=k):
                    remote(
                        served_far.at[pl.ds(dy * CHUNK + k * CAP, CAP)],
                        embedded.at[pl.ds(pl.multiple_of(far_base + k * CAP, CAP), CAP)],
                        far_row_send, row_recv.at[far_group],
                        device(z, x - k // 2, c - k % 2, y + dy),
                    ).start()

    for dy in (1, 3, 2):
        block = (y - dy + 4) % 4
        remote(normed.at[block], normed.at[block], ring_send, ring_recv.at[dy - 1], up).wait_recv()
        project_keys(block)

    def emit(source, target, index):
        copy = pltpu.make_async_copy(source, target, out_sem.at[index])
        copy.start()
        return copy

    emitted = [emit(keys, keys_done, 0), emit(values, values_done, 1)]

    group_base = me * KEYS
    second = row_start[1] - group_base
    end_first, end_second = row_start[0] - group_base + hist_len[0], second + hist_len[1]

    def locate(spot):
        user = (spot >= second).astype(I32)
        return user, spot < jnp.where(user == 1, end_second, end_first)

    key_spot = iota((1, KEYS), 1)
    key_user, key_live = locate(key_spot)
    query_spot = y * ROWS + iota((ROWS, 1), 0)
    query_user, query_live = locate(query_spot)

    def attend(rows, query):
        def head(h, carry):
            columns = pl.ds(pl.multiple_of(h * HEAD_DIM, HEAD_DIM), HEAD_DIM)
            scores = dot_nt(query[:, columns], keys[:, columns])
            weights = half_silu(scores * scale_mask[0:rows, :]).astype(BF16)
            attended[0:rows, columns] = dot(weights, values[:, columns])
            return carry

        lax.fori_loop(0, HEADS, head, 0, unroll=4)

    def finish(rows, residual, gate, write):
        mixed = (layer_norm(attended[0:rows, :], gain_attn[...]) * gate[...].astype(F32)).astype(BF16)
        for n in range(WIDTH // 256):
            columns = pl.ds(n * 256, 256)
            write(columns, (residual(columns) + dot(mixed, wout[:, columns])).astype(BF16))

    allowed = (
        (query_user == key_user)
        & (query_live & key_live)
        & (key_spot <= query_spot)
    )
    scale_mask[...] = jnp.where(allowed, half_scale, 0.0)
    attend(ROWS, hquery)

    def write_hist(columns, out):
        hist[:, columns] = out

    finish(ROWS, lambda columns: tokens[:, columns].astype(F32), hgate, write_hist)

    emitted.append(emit(hist, hist_done, 2))

    def pick_rows(first, count):
        def part(n, carry):
            rows = pl.ds(pl.multiple_of(n * 256, 256), 256)
            pick = (iota((256, count), 1) + first == place[rows, 0:1]).astype(BF16)
            for m in range(WIDTH // 256):
                columns = pl.ds(m * 256, 256)
                found = dot(pick, embedded[pl.ds(first, count), columns])
                if first:
                    found = found + rows_in[rows, columns]
                rows_in[rows, columns] = found
            return carry

        lax.fori_loop(0, CANDS // 256, part, 0)

    for q in range(NEAR):
        rows = pl.ds(CAP, CHUNK - CAP) if q == 0 else pl.ds(q * CHUNK, CHUNK)
        remote(embedded.at[rows], embedded.at[rows], row_send, row_recv.at[q], up).wait_recv()
    pick_rows(0, NEAR * CHUNK)
    for q in range(NEAR, 8):
        own_copy = (z + group_dz(q)) % 4 == y

        @pl.when(own_copy)
        def _(q=q):
            rows = pl.ds(q * CHUNK + CAP, CHUNK - CAP)
            remote(embedded.at[rows], embedded.at[rows], row_send, row_recv.at[q], up).wait_recv()

        @pl.when(jnp.logical_not(own_copy))
        def _(q=q):
            rows = pl.ds(q * CHUNK, CHUNK)
            remote(embedded.at[rows], embedded.at[rows], row_send, row_recv.at[q], up).wait_recv()

    pick_rows(NEAR * CHUNK, (8 - NEAR) * CHUNK)

    def norm_rows(n, carry):
        rows = pl.ds(pl.multiple_of(n * CHUNK, CHUNK), CHUNK)
        value = rows_in[rows, :]
        rows_out[rows, :] = value.astype(BF16)
        cnormed[rows, :] = layer_norm(value, gain_in[...]).astype(BF16)
        return carry

    lax.fori_loop(0, CANDS // CHUNK, norm_rows, 0)
    emitted.append(emit(rows_out, rows_done, 3))

    def write_cquery(columns, out):
        cquery[:, columns] = out.astype(BF16)

    def write_cgate(columns, out):
        cgate[:, columns] = half_silu(out * 0.5).astype(BF16)

    project(lambda: cnormed[...], 2, write_cquery)
    emitted.append(emit(cquery, query_done, 4))
    project(lambda: cnormed[...], 0, write_cgate)
    emitted.append(emit(cgate, gate_done, 5))

    others = normed.at[pl.ds(0, 3)]
    remote(others, others, ring_send, ring_recv.at[0], up).wait_send()
    lots = requests.at[pl.ds(0, OWNERS - 2)]
    remote(lots, lots, req_send, req_recv.at[0], up).wait_send()

    @pl.when(jnp.logical_not(is_holder))
    def _():
        remote(requests.at[0], requests.at[0], req_send, req_recv.at[0], up).wait_send()

    rows = served.at[pl.ds(CAP, NEAR * CHUNK - CAP)]
    remote(rows, rows, row_send, row_recv.at[0], up).wait_send()

    @pl.when(is_holder)
    def _():
        rows = served_far.at[pl.ds(CAP, 4 * CHUNK - CAP)]
        remote(rows, rows, far_row_send, row_recv.at[0], up).wait_send()

    @pl.when(phase == 0)
    def _():
        remote(far_table, far_table, copy_up, copy_recv.at[0], z_up).wait_send()
        remote(far_table, far_table, copy_down, copy_recv.at[0], z_down).wait_send()

    @pl.when(phase == 3)
    def _():
        half = far_table.at[first_half]
        remote(half, half, copy_up, copy_recv.at[0], z_up).wait_send()

    @pl.when(phase == 1)
    def _():
        half = far_table.at[last_half]
        remote(half, half, copy_down, copy_recv.at[0], z_down).wait_send()

    for copy in emitted:
        copy.wait()


def candidate_kernel(
    hist_len, row_start, base, hist, keys_in, values_in, rows_in, gate_in, query_in, w_out, gain_attn,
    hist_out, cand_out,
    keys, values, rows, gate, query, wout, attended, result, hist_held, sem, out_sem,
):
    half_scale = 0.5 / math.sqrt(HEAD_DIM)
    hist_copy = pltpu.make_async_copy(hist, hist_held, sem.at[6])
    loads = [
        pltpu.make_async_copy(source, target, sem.at[n])
        for n, (source, target) in enumerate(
            [(query_in, query), (keys_in, keys), (values_in, values), (gate_in, gate), (w_out, wout), (rows_in, rows)]
        )
    ]
    for copy in loads:
        copy.start()
    hist_copy.start()
    second = row_start[1] - base[0]
    starts = (0, second)
    ends = (row_start[0] - base[0] + hist_len[0], second + hist_len[1])
    tiles = ((0, (second + 255) // 256), (second // 256, KEYS // 256))
    stores = []
    for copy in loads[:3]:
        copy.wait()
    for user in range(2):
        own = pl.ds(user * 256, 256)
        attended[...] = jnp.zeros_like(attended)

        def tile(t, carry, user=user, own=own):
            first = pl.multiple_of(t * 256, 256)
            spot = first + iota((1, 256), 1)
            live = (spot >= starts[user]) & (spot < ends[user])
            scale = jnp.where(live, half_scale, 0.0)
            span = pl.ds(first, 256)
            for h in range(HEADS):
                columns = pl.ds(h * HEAD_DIM, HEAD_DIM)
                scores = dot_nt(query[own, columns], keys[span, columns])
                weights = half_silu(scores * scale).astype(BF16)
                attended[:, columns] += dot(weights, values[span, columns])
            return carry

        lax.fori_loop(tiles[user][0], tiles[user][1], tile, 0)
        if user == 0:
            for copy in loads[3:]:
                copy.wait()
            hist_copy.wait()
            stores.append(pltpu.make_async_copy(hist_held, hist_out, out_sem.at[2]))
            stores[-1].start()
        mixed = (layer_norm(attended[...], gain_attn[...]) * gate[own, :].astype(F32)).astype(BF16)
        for n in range(WIDTH // 256):
            columns = pl.ds(n * 256, 256)
            result[user, :, columns] = (
                rows[own, columns].astype(F32) + dot(mixed, wout[:, columns])
            ).astype(BF16)
        stores.append(pltpu.make_async_copy(result.at[user], cand_out.at[user], out_sem.at[user]))
        stores[-1].start()
    for copy in stores:
        copy.wait()


def body(
    tokens, item_table, w_in, w_out, gain_in, gain_attn, hist_len, row_start, impressions, item_slot
):
    vmem = pl.BlockSpec(memory_space=pltpu.VMEM)
    smem = pl.BlockSpec(memory_space=pltpu.SMEM)
    anywhere = pl.BlockSpec(memory_space=pl.ANY)
    gain_attn_row = gain_attn.reshape(1, WIDTH)
    big = jax.ShapeDtypeStruct((KEYS, WIDTH), BF16)
    half = jax.ShapeDtypeStruct((CANDS, WIDTH), BF16)
    hist, keys, values, rows, gate, query = pl.pallas_call(
        kernel,
        out_shape=(jax.ShapeDtypeStruct((ROWS, WIDTH), BF16), big, big, half, half, half),
        in_specs=[smem, smem, vmem, vmem, anywhere, anywhere, vmem, vmem, vmem, vmem],
        out_specs=(anywhere,) * 6,
        scratch_shapes=[
            pltpu.VMEM((4, WIDTH, WIDTH), BF16),
            pltpu.VMEM((WIDTH, WIDTH), BF16),
            pltpu.VMEM((4, ROWS, WIDTH), BF16),
            pltpu.VMEM((KEYS, WIDTH), BF16),
            pltpu.VMEM((KEYS, WIDTH), BF16),
            pltpu.VMEM((ROWS, WIDTH), BF16),
            pltpu.VMEM((ROWS, WIDTH), BF16),
            pltpu.VMEM((ROWS, WIDTH), F32),
            pltpu.VMEM((ROWS, KEYS), F32),
            pltpu.VMEM((ROWS, WIDTH), BF16),
            pltpu.VMEM((OWNERS, 1, 128), I32),
            pltpu.VMEM((NEAR * 8, 1, 128), I32),
            pltpu.VMEM((32, 1, 128), I32),
            pltpu.VMEM((ROWS, WIDTH), BF16),
            pltpu.VMEM((NEAR * CHUNK, WIDTH), BF16),
            pltpu.VMEM((4 * CHUNK, WIDTH), BF16),
            pltpu.VMEM((OWNERS * CAP, WIDTH), BF16),
            pltpu.VMEM((CANDS, WIDTH), F32),
            pltpu.VMEM((CANDS, WIDTH), BF16),
            pltpu.VMEM((CANDS, WIDTH), BF16),
            pltpu.VMEM((CANDS, WIDTH), BF16),
            pltpu.VMEM((CANDS, WIDTH), BF16),
            pltpu.VMEM((CANDS, 128), I32),
            pltpu.SemaphoreType.DMA((5,)),
            pltpu.SemaphoreType.DMA,
            pltpu.SemaphoreType.DMA((NEAR,)),
            pltpu.SemaphoreType.DMA,
            pltpu.SemaphoreType.DMA,
            pltpu.SemaphoreType.DMA,
            pltpu.SemaphoreType.DMA((8,)),
            pltpu.SemaphoreType.DMA,
            pltpu.SemaphoreType.DMA((3,)),
            pltpu.SemaphoreType.DMA,
            pltpu.SemaphoreType.DMA,
            pltpu.SemaphoreType.DMA((2,)),
            pltpu.SemaphoreType.DMA((6,)),
        ],
        compiler_params=pltpu.CompilerParams(
            collective_id=0, has_side_effects=True, vmem_limit_bytes=56 * 2**20
        ),
    )(
        hist_len, row_start, tokens, item_table, w_in, w_out,
        gain_in.reshape(1, WIDTH), gain_attn_row,
        impressions, item_slot.reshape(128, 128),
    )
    base = (lax.axis_index("users") * KEYS).astype(I32).reshape(1)
    return pl.pallas_call(
        candidate_kernel,
        out_shape=(
            jax.ShapeDtypeStruct((ROWS, WIDTH), BF16),
            jax.ShapeDtypeStruct((2, CANDS // 2, WIDTH), BF16),
        ),
        in_specs=[smem, smem, smem] + [anywhere] * 7 + [vmem],
        out_specs=(anywhere, anywhere),
        scratch_shapes=[
            pltpu.VMEM((KEYS, WIDTH), BF16),
            pltpu.VMEM((KEYS, WIDTH), BF16),
            pltpu.VMEM((CANDS, WIDTH), BF16),
            pltpu.VMEM((CANDS, WIDTH), BF16),
            pltpu.VMEM((CANDS, WIDTH), BF16),
            pltpu.VMEM((WIDTH, WIDTH), BF16),
            pltpu.VMEM((CANDS // 2, WIDTH), F32),
            pltpu.VMEM((2, CANDS // 2, WIDTH), BF16),
            pltpu.VMEM((ROWS, WIDTH), BF16),
            pltpu.SemaphoreType.DMA((7,)),
            pltpu.SemaphoreType.DMA((3,)),
        ],
        compiler_params=pltpu.CompilerParams(vmem_limit_bytes=56 * 2**20),
    )(hist_len, row_start, base, hist, keys, values, rows, gate, query, w_out, gain_attn_row)


def solution(mesh):
    placed = (
        P(("users", "seq"), None),
        P("users", None),
        P(),
        P(),
        P(),
        P(),
        P("users"),
        P("users"),
        P("users", "seq"),
        P(),
    )
    return jax.shard_map(
        body,
        mesh=mesh,
        in_specs=placed,
        out_specs=(P(("users", "seq"), None), P("users", "seq", None)),
        check_vma=False,
    )
```

time: 87.1 us -> 74.7 us (0.86)
  the two profiles are of different devices: /device:TPU:49 before, /device:TPU:64 now
where the time goes in v2:
time: 74.7 us; the launch traced here: 74.6 us
  Pallas kernels  73.9 us (99%)
    pallas_call x1, Pallas kernels, body(): pl.pallas_call(kernel, out_shape=(jax.ShapeDtypeStruct((ROWS, WIDTH), BF1...  62.7 us
    pallas_call x1, Pallas kernels, body(): pl.pallas_call(candidate_kernel, out_shape=(jax.ShapeDtypeStruct((ROWS, W...  11.2 us

profile of v2, /device:TPU:64, one launch (start us, length us, event | category | flops | bytes accessed | tf_op | source)
XLA Modules:
  0.0 74.6 jit_solution(10824366469908593490)
XLA Ops:
  0.6 62.7 %shard_map.113 = (bf16[256,1024]{1,0:T(8,128)(2,1)}, bf16[1024,1024]{1,0:T(8,128)(2,1)}, bf16[1024,1024]{1,0:T(8,128)(2,1)}, bf16[512,1024]{1,0:T(8,128)(2,1)}, ...) custom-call(s32[2]{0:T(128)} %hist_len.3, s32[2]{0:T(128)} %row_start.3, bf16[256,1024]{1,0:T(8,128)(2,1)} %tokens.1, ...), custom_call_target="tpu_custom_call" | custom-call | tf_op jit(solution)/shard_map/pallas_call | solution.py:507
  63.4 11.2 %shard_map.114 = (bf16[256,1024]{1,0:T(8,128)(2,1)}, bf16[2,256,1024]{2,1,0:T(8,128)(2,1)}) custom-call(s32[2]{0:T(128)} %hist_len.3, s32[2]{0:T(128)} %row_start.3, s32[1]{0:T(128)} %bitcast.base, bf16[256,1024]{1,0:T(8,128)(2,1)} %get-tuple-element.8.hist, bf16[1024,1024]{1,0:T(8,128)(2,1)} %get-tuple-element.9.keys_in, ...), custom_call_target="tpu_custom_call" | custom-call | tf_op jit(solution)/shard_map/pallas_call | solution.py:559

commit v3 on v2

--- a/solution.py
+++ b/solution.py
@@ -61,10 +61,10 @@
 
 def kernel(
     hist_len, row_start, tokens, table, w_in, w_out, gain_in, gain_attn, wanted, item_slot,
-    hist_done, keys_done, values_done, rows_done, gate_done, query_done,
+    hist_done, rows_done, mixed_done,
     win, wout, normed, keys, values, hgate, hquery, attended, scale_mask, hist,
     requests, asked, asked_far, far_table, served, served_far, embedded,
-    rows_in, rows_out, cnormed, cgate, cquery, place,
+    rows_in, rows_out, cnormed, cgate, cquery, cattended, cmixed, place,
     w_sem, req_send, req_recv, far_req_recv, row_send, far_row_send, row_recv,
     ring_send, ring_recv, copy_up, copy_down, copy_recv, out_sem,
 ):
@@ -127,8 +127,6 @@
         requests[j] = request_rows[j : j + 1, :]
     asked[0] = request_rows[0:1, :]
 
-    normed[y] = layer_norm(tokens[...].astype(F32), gain_in[...]).astype(BF16)
-
     pl.semaphore_wait(barrier, 65)
 
     for q in range(8):
@@ -176,6 +174,7 @@
 
     up = device(z, x, c, y + 1)
     own = normed.at[y]
+    normed[y] = layer_norm(tokens[...].astype(F32), gain_in[...]).astype(BF16)
     for dy in (1, 3, 2):
         remote(own, own, ring_send, ring_recv.at[dy - 1], device(z, x, c, y + dy)).start()
 
@@ -227,7 +226,7 @@
             write(columns, dot(rows_value(), win[block, :, columns]))
             return carry
 
-        lax.fori_loop(0, WIDTH // 256, step, 0)
+        lax.fori_loop(0, WIDTH // 256, step, 0, unroll=4)
 
     def project_keys(block):
         rows = pl.ds(pl.multiple_of(block * ROWS, ROWS), ROWS)
@@ -300,7 +299,7 @@
         copy.start()
         return copy
 
-    emitted = [emit(keys, keys_done, 0), emit(values, values_done, 1)]
+    emitted = []
 
     group_base = me * KEYS
     second = row_start[1] - group_base
@@ -344,7 +343,7 @@
 
     finish(ROWS, lambda columns: tokens[:, columns].astype(F32), hgate, write_hist)
 
-    emitted.append(emit(hist, hist_done, 2))
+    emitted.append(emit(hist, hist_done, 0))
 
     def pick_rows(first, count):
         def part(n, carry):
@@ -387,7 +386,7 @@
         return carry
 
     lax.fori_loop(0, CANDS // CHUNK, norm_rows, 0)
-    emitted.append(emit(rows_out, rows_done, 3))
+    emitted.append(emit(rows_out, rows_done, 1))
 
     def write_cquery(columns, out):
         cquery[:, columns] = out.astype(BF16)
@@ -396,9 +395,58 @@
         cgate[:, columns] = half_silu(out * 0.5).astype(BF16)
 
     project(lambda: cnormed[...], 2, write_cquery)
-    emitted.append(emit(cquery, query_done, 4))
+
+    lanes = iota((1, HEAD_DIM), 1)
+    tile_lanes = iota((1, 256), 1)
+    to_second = [(lanes * 0 + t * 256 >= second).astype(F32) for t in range(4)]
+    to_first = [(lanes * 0 + t * 256 < second).astype(F32) for t in range(4)]
+    shared = second >> 8
+    is_shared = [(lanes * 0 + t == shared).astype(F32).astype(BF16) for t in range(4)]
+
+    def tile_scale(spot, second_rows):
+        low = jnp.where(second_rows, second, 0)
+        high = jnp.where(second_rows, end_second, end_first)
+        return jnp.where((spot >= low) & (spot < high), half_scale, 0.0)
+
+    scales = [tile_scale(tile_lanes + t * 256, tile_lanes * 0 + t * 256 >= second) for t in range(4)]
+    shared_spot = tile_lanes + shared * 256
+    shared_live = (shared_spot >= second) & (shared_spot < end_second) & (tile_lanes * 0 + shared * 256 < second)
+    shared_scale = jnp.where(shared_live, half_scale, 0.0)
+
+    def cand_head(h, carry):
+        columns = pl.ds(pl.multiple_of(h * HEAD_DIM, HEAD_DIM), HEAD_DIM)
+        first_query, second_query = cquery[0:256, columns], cquery[256:512, columns]
+
+        def weigh(query, key, value, scale):
+            return dot(half_silu(dot_nt(query, key) * scale).astype(BF16), value)
+
+        key_shared = value_shared = None
+        for t in range(4):
+            span = pl.ds(t * 256, 256)
+            key, value = keys[span, columns], values[span, columns]
+            if t == 0:
+                key_shared, value_shared = key * is_shared[t], value * is_shared[t]
+                cattended[0:256, columns] = weigh(first_query, key, value, scales[t])
+                continue
+            key_shared = key_shared + key * is_shared[t]
+            value_shared = value_shared + value * is_shared[t]
+            query = first_query * to_first[t].astype(BF16) + second_query * to_second[t].astype(BF16)
+            found = weigh(query, key, value, scales[t])
+            cattended[0:256, columns] += found * to_first[t]
+            if t == 1:
+                cattended[256:512, columns] = found * to_second[t]
+            else:
+                cattended[256:512, columns] += found * to_second[t]
+        cattended[256:512, columns] += weigh(second_query, key_shared, value_shared, shared_scale)
+        return carry
+
+    lax.fori_loop(0, HEADS, cand_head, 0, unroll=4)
     project(lambda: cnormed[...], 0, write_cgate)
-    emitted.append(emit(cgate, gate_done, 5))
+    for n in range(4):
+        rows = pl.ds(n * CHUNK, CHUNK)
+        mixed = layer_norm(cattended[rows, :], gain_attn[...]) * cgate[rows, :].astype(F32)
+        cmixed[rows, :] = mixed.astype(BF16)
+        emitted.append(emit(cmixed.at[rows], mixed_done.at[rows], 2 + n))
 
     others = normed.at[pl.ds(0, 3)]
     remote(others, others, ring_send, ring_recv.at[0], up).wait_send()
@@ -436,61 +484,39 @@
         copy.wait()
 
 
-def candidate_kernel(
-    hist_len, row_start, base, hist, keys_in, values_in, rows_in, gate_in, query_in, w_out, gain_attn,
-    hist_out, cand_out,
-    keys, values, rows, gate, query, wout, attended, result, hist_held, sem, out_sem,
+def output_kernel(
+    hist, mixed_in, rows_in, w_out, hist_out, cand_out, wout, hist_held, mixed, rows, result, sem, out_sem
 ):
-    half_scale = 0.5 / math.sqrt(HEAD_DIM)
-    hist_copy = pltpu.make_async_copy(hist, hist_held, sem.at[6])
-    loads = [
-        pltpu.make_async_copy(source, target, sem.at[n])
-        for n, (source, target) in enumerate(
-            [(query_in, query), (keys_in, keys), (values_in, values), (gate_in, gate), (w_out, wout), (rows_in, rows)]
+    def load(source, target, index):
+        copy = pltpu.make_async_copy(source, target, sem.at[index])
+        copy.start()
+        return copy
+
+    first_load = load(w_out, wout, 9)
+    loads = []
+    for n in range(4):
+        part = pl.ds(n * CHUNK, CHUNK)
+        loads.append(
+            (load(mixed_in.at[part], mixed.at[part], 2 * n), load(rows_in.at[part], rows.at[part], 2 * n + 1))
         )
-    ]
-    for copy in loads:
+    hist_load = load(hist, hist_held, 8)
+    stores = []
+
+    def store(source, target, index):
+        copy = pltpu.make_async_copy(source, target, out_sem.at[index])
         copy.start()
-    hist_copy.start()
-    second = row_start[1] - base[0]
-    starts = (0, second)
-    ends = (row_start[0] - base[0] + hist_len[0], second + hist_len[1])
-    tiles = ((0, (second + 255) // 256), (second // 256, KEYS // 256))
-    stores = []
-    for copy in loads[:3]:
-        copy.wait()
-    for user in range(2):
-        own = pl.ds(user * 256, 256)
-        attended[...] = jnp.zeros_like(attended)
-
-        def tile(t, carry, user=user, own=own):
-            first = pl.multiple_of(t * 256, 256)
-            spot = first + iota((1, 256), 1)
-            live = (spot >= starts[user]) & (spot < ends[user])
-            scale = jnp.where(live, half_scale, 0.0)
-            span = pl.ds(first, 256)
-            for h in range(HEADS):
-                columns = pl.ds(h * HEAD_DIM, HEAD_DIM)
-                scores = dot_nt(query[own, columns], keys[span, columns])
-                weights = half_silu(scores * scale).astype(BF16)
-                attended[:, columns] += dot(weights, values[span, columns])
-            return carry
-
-        lax.fori_loop(tiles[user][0], tiles[user][1], tile, 0)
-        if user == 0:
-            for copy in loads[3:]:
-                copy.wait()
-            hist_copy.wait()
-            stores.append(pltpu.make_async_copy(hist_held, hist_out, out_sem.at[2]))
-            stores[-1].start()
-        mixed = (layer_norm(attended[...], gain_attn[...]) * gate[own, :].astype(F32)).astype(BF16)
-        for n in range(WIDTH // 256):
-            columns = pl.ds(n * 256, 256)
-            result[user, :, columns] = (
-                rows[own, columns].astype(F32) + dot(mixed, wout[:, columns])
-            ).astype(BF16)
-        stores.append(pltpu.make_async_copy(result.at[user], cand_out.at[user], out_sem.at[user]))
-        stores[-1].start()
+        stores.append(copy)
+
+    first_load.wait()
+    for n in range(4):
+        for copy in loads[n]:
+            copy.wait()
+        part = pl.ds(n * CHUNK, CHUNK)
+        result[part, :] = (rows[part, :].astype(F32) + dot(mixed[part, :], wout[...])).astype(BF16)
+        store(result.at[part], cand_out.at[n // 2, pl.ds(n % 2 * CHUNK, CHUNK)], n)
+        if n == 0:
+            hist_load.wait()
+            store(hist_held, hist_out, 4)
     for copy in stores:
         copy.wait()
 
@@ -501,14 +527,12 @@
     vmem = pl.BlockSpec(memory_space=pltpu.VMEM)
     smem = pl.BlockSpec(memory_space=pltpu.SMEM)
     anywhere = pl.BlockSpec(memory_space=pl.ANY)
-    gain_attn_row = gain_attn.reshape(1, WIDTH)
-    big = jax.ShapeDtypeStruct((KEYS, WIDTH), BF16)
     half = jax.ShapeDtypeStruct((CANDS, WIDTH), BF16)
-    hist, keys, values, rows, gate, query = pl.pallas_call(
+    hist, rows, mixed = pl.pallas_call(
         kernel,
-        out_shape=(jax.ShapeDtypeStruct((ROWS, WIDTH), BF16), big, big, half, half, half),
+        out_shape=(jax.ShapeDtypeStruct((ROWS, WIDTH), BF16), half, half),
         in_specs=[smem, smem, vmem, vmem, anywhere, anywhere, vmem, vmem, vmem, vmem],
-        out_specs=(anywhere,) * 6,
+        out_specs=(anywhere,) * 3,
         scratch_shapes=[
             pltpu.VMEM((4, WIDTH, WIDTH), BF16),
             pltpu.VMEM((WIDTH, WIDTH), BF16),
@@ -531,6 +555,8 @@
             pltpu.VMEM((CANDS, WIDTH), BF16),
             pltpu.VMEM((CANDS, WIDTH), BF16),
             pltpu.VMEM((CANDS, WIDTH), BF16),
+            pltpu.VMEM((CANDS, WIDTH), BF16),
+            pltpu.VMEM((CANDS, WIDTH), F32),
             pltpu.VMEM((CANDS, WIDTH), BF16),
             pltpu.VMEM((CANDS, 128), I32),
             pltpu.SemaphoreType.DMA((5,)),
@@ -552,33 +578,28 @@
         ),
     )(
         hist_len, row_start, tokens, item_table, w_in, w_out,
-        gain_in.reshape(1, WIDTH), gain_attn_row,
+        gain_in.reshape(1, WIDTH), gain_attn.reshape(1, WIDTH),
         impressions, item_slot.reshape(128, 128),
     )
-    base = (lax.axis_index("users") * KEYS).astype(I32).reshape(1)
     return pl.pallas_call(
-        candidate_kernel,
+        output_kernel,
         out_shape=(
             jax.ShapeDtypeStruct((ROWS, WIDTH), BF16),
             jax.ShapeDtypeStruct((2, CANDS // 2, WIDTH), BF16),
         ),
-        in_specs=[smem, smem, smem] + [anywhere] * 7 + [vmem],
+        in_specs=[anywhere] * 4,
         out_specs=(anywhere, anywhere),
         scratch_shapes=[
-            pltpu.VMEM((KEYS, WIDTH), BF16),
-            pltpu.VMEM((KEYS, WIDTH), BF16),
-            pltpu.VMEM((CANDS, WIDTH), BF16),
-            pltpu.VMEM((CANDS, WIDTH), BF16),
-            pltpu.VMEM((CANDS, WIDTH), BF16),
             pltpu.VMEM((WIDTH, WIDTH), BF16),
-            pltpu.VMEM((CANDS // 2, WIDTH), F32),
-            pltpu.VMEM((2, CANDS // 2, WIDTH), BF16),
             pltpu.VMEM((ROWS, WIDTH), BF16),
-            pltpu.SemaphoreType.DMA((7,)),
-            pltpu.SemaphoreType.DMA((3,)),
+            pltpu.VMEM((CANDS, WIDTH), BF16),
+            pltpu.VMEM((CANDS, WIDTH), BF16),
+            pltpu.VMEM((CANDS, WIDTH), BF16),
+            pltpu.SemaphoreType.DMA((10,)),
+            pltpu.SemaphoreType.DMA((5,)),
         ],
         compiler_params=pltpu.CompilerParams(vmem_limit_bytes=56 * 2**20),
-    )(hist_len, row_start, base, hist, keys, values, rows, gate, query, w_out, gain_attn_row)
+    )(hist, mixed, rows, w_out)
 
 
 def solution(mesh):

time: 74.7 us -> 72.9 us (0.976)
  Pallas kernels: 73.9 us -> 71.3 us
    pallas_call x1, Pallas kernels: 11.2 us -> 4.53 us  [body(): pl.pallas_call(output_kernel, out_shape=(jax.ShapeDtypeStruct((ROWS, WIDT...]
    pallas_call x1, Pallas kernels: 62.7 us -> 66.8 us  [body(): pl.pallas_call(kernel, out_shape=(jax.ShapeDtypeStruct((ROWS, WIDTH), BF1...]
where the time goes in v3:
time: 72.9 us; the launch traced here: 72.1 us
  Pallas kernels  71.3 us (98%)
  between operations  0.8 us (1%)
    pallas_call x1, Pallas kernels, body(): pl.pallas_call(kernel, out_shape=(jax.ShapeDtypeStruct((ROWS, WIDTH), BF1...  66.8 us
    pallas_call x1, Pallas kernels, body(): pl.pallas_call(output_kernel, out_shape=(jax.ShapeDtypeStruct((ROWS, WIDT...  4.53 us

profile of v3, /device:TPU:64, one launch (start us, length us, event | category | flops | bytes accessed | tf_op | source)
XLA Modules:
  0.0 72.1 jit_solution(12930427080301299728)
XLA Ops:
  0.6 66.8 %shard_map.113 = (bf16[256,1024]{1,0:T(8,128)(2,1)}, bf16[512,1024]{1,0:T(8,128)(2,1)}, bf16[512,1024]{1,0:T(8,128)(2,1)}) custom-call(s32[2]{0:T(128)} %hist_len.1, s32[2]{0:T(128)} %row_start.1, bf16[256,1024]{1,0:T(8,128)(2,1)} %tokens.1, bf16[256,1024]{1,0:T(8,128)(2,1)} %table.1, bf16[1024,4096]{1,0:T(8,128)(2,1)} %w_in.1, bf16[1024,1024]{1,0:T(8,128)(2,1)} %w_out.3, ...), custom_call_target="tpu_custom_call" | custom-call | tf_op jit(solution)/shard_map/pallas_call | solution.py:531
  67.4 4.5 %shard_map.114 = (bf16[256,1024]{1,0:T(8,128)(2,1)}, bf16[2,256,1024]{2,1,0:T(8,128)(2,1)}) custom-call(bf16[256,1024]{1,0:T(8,128)(2,1)} %get-tuple-element.5.hist, bf16[512,1024]{1,0:T(8,128)(2,1)} %get-tuple-element.6.mixed_in, bf16[512,1024]{1,0:T(8,128)(2,1)} %get-tuple-element.7.rows_in, bf16[1024,1024]{1,0:T(8,128)(2,1)} %w_out.3), custom_call_target="tpu_custom_call" | custom-call | tf_op jit(solution)/shard_map/pallas_call | solution.py:584

commit v4 on v3

--- a/solution.py
+++ b/solution.py
@@ -101,6 +101,23 @@
             greet(device(z, x + k // 2, c + k % 2, y + dy))
     greet(device(z + 3, x, c, y))
     greet(device(z + 5, x, c, y))
+
+    pl.semaphore_wait(barrier, 65)
+
+    phase = (z + 8 - y) % 4
+    is_holder = phase != 2
+    first_half, last_half = pl.ds(0, ROWS // 2), pl.ds(ROWS // 2, ROWS // 2)
+    z_up, z_down = device(z + 1, x, c, y), device(z - 1, x, c, y)
+
+    def copy_half(rows, send, index, plane):
+        remote(
+            table.at[rows], far_table.at[rows], send, copy_recv.at[index], device(plane, x, c, y)
+        ).start()
+
+    @pl.when(phase == 0)
+    def _():
+        copy_half(first_half, copy_up, 0, z + 3)
+        copy_half(last_half, copy_down, 0, z - 3)
 
     ids = jnp.concatenate([wanted[0:1, :], wanted[1:2, :]], axis=1)
     pick_high = (iota((128, CANDS), 0) == (ids >> 7)).astype(BF16)
@@ -127,8 +144,6 @@
         requests[j] = request_rows[j : j + 1, :]
     asked[0] = request_rows[0:1, :]
 
-    pl.semaphore_wait(barrier, 65)
-
     for q in range(8):
         dz = group_dz(q)
         if q < NEAR:
@@ -159,18 +174,10 @@
                     def _(j=j):
                         asked_far[y * 8] = requests[j]
 
-    phase = (z + 8 - y) % 4
-    is_holder = phase != 2
-    first_half, last_half = pl.ds(0, ROWS // 2), pl.ds(ROWS // 2, ROWS // 2)
-    z_up, z_down = device(z + 1, x, c, y), device(z - 1, x, c, y)
-
     @pl.when(phase == 0)
     def _():
-        far_up, far_down = device(z + 3, x, c, y), device(z - 3, x, c, y)
-        remote(table.at[first_half], far_table.at[first_half], copy_up, copy_recv.at[0], far_up).start()
-        remote(table.at[last_half], far_table.at[last_half], copy_down, copy_recv.at[0], far_down).start()
-        remote(table.at[last_half], far_table.at[last_half], copy_up, copy_recv.at[1], far_up).start()
-        remote(table.at[first_half], far_table.at[first_half], copy_down, copy_recv.at[1], far_down).start()
+        copy_half(last_half, copy_up, 1, z + 3)
+        copy_half(first_half, copy_down, 1, z - 3)
 
     up = device(z, x, c, y + 1)
     own = normed.at[y]
@@ -246,12 +253,6 @@
     def write_hquery(columns, out):
         hquery[:, columns] = out.astype(BF16)
 
-    for copy in weight_copies:
-        copy.wait()
-    project(lambda: normed[y], 0, write_hgate)
-    project(lambda: normed[y], 2, write_hquery)
-    project_keys(y)
-
     @pl.when(phase == 0)
     def _():
         half, other = far_table.at[first_half], far_table.at[last_half]
@@ -288,6 +289,12 @@
                         far_row_send, row_recv.at[far_group],
                         device(z, x - k // 2, c - k % 2, y + dy),
                     ).start()
+
+    for copy in weight_copies:
+        copy.wait()
+    project(lambda: normed[y], 0, write_hgate)
+    project(lambda: normed[y], 2, write_hquery)
+    project_keys(y)
 
     for dy in (1, 3, 2):
         block = (y - dy + 4) % 4

time: 72.9 us -> 73 us (level)
  no operation moved by 1% of the time
where the time goes in v4:
time: 73 us; the launch traced here: 72.1 us
  Pallas kernels  71.3 us (98%)
  between operations  0.8 us (1%)
    pallas_call x1, Pallas kernels, body(): pl.pallas_call(kernel, out_shape=(jax.ShapeDtypeStruct((ROWS, WIDTH), BF1...  66.8 us
    pallas_call x1, Pallas kernels, body(): pl.pallas_call(output_kernel, out_shape=(jax.ShapeDtypeStruct((ROWS, WIDT...  4.52 us

profile of v4, /device:TPU:64, one launch (start us, length us, event | category | flops | bytes accessed | tf_op | source)
XLA Modules:
  0.0 72.1 jit_solution(5811963887200373627)
XLA Ops:
  0.6 66.8 %shard_map.113 = (bf16[256,1024]{1,0:T(8,128)(2,1)}, bf16[512,1024]{1,0:T(8,128)(2,1)}, bf16[512,1024]{1,0:T(8,128)(2,1)}) custom-call(s32[2]{0:T(128)} %hist_len.1, s32[2]{0:T(128)} %row_start.1, bf16[256,1024]{1,0:T(8,128)(2,1)} %tokens.1, bf16[256,1024]{1,0:T(8,128)(2,1)} %table.1, bf16[1024,4096]{1,0:T(8,128)(2,1)} %w_in.1, bf16[1024,1024]{1,0:T(8,128)(2,1)} %w_out.3, ...), custom_call_target="tpu_custom_call" | custom-call | tf_op jit(solution)/shard_map/pallas_call | solution.py:538
  67.4 4.5 %shard_map.114 = (bf16[256,1024]{1,0:T(8,128)(2,1)}, bf16[2,256,1024]{2,1,0:T(8,128)(2,1)}) custom-call(bf16[256,1024]{1,0:T(8,128)(2,1)} %get-tuple-element.5.hist, bf16[512,1024]{1,0:T(8,128)(2,1)} %get-tuple-element.6.mixed_in, bf16[512,1024]{1,0:T(8,128)(2,1)} %get-tuple-element.7.rows_in, bf16[1024,1024]{1,0:T(8,128)(2,1)} %w_out.3), custom_call_target="tpu_custom_call" | custom-call | tf_op jit(solution)/shard_map/pallas_call | solution.py:591
